TPU v7x, 512 devices: a whole 4x4x16 slice. The times are simulated.
512 devices in a mesh: people: 32 (over z, core), var: 16 (over y, x).
Axes of the slice: x: 4, y: 4, z: 16, core: 2. Of those that a mesh axis runs over, the one named last changes fastest.
Arguments:
- genotype: int32 [16384, 16384], P('people', 'var'), may hold values from 0 to 2
- dosage_mean: float32 [16384], P('var'), may hold values from 0.6 to 1.4
- residual: float32 [4, 16384], P(None, 'people'), may hold values from -10.5 to 10.5, as said below
- latent_old: float32 [4, 16, 16384], P(None, 'var'), may hold values from -3 to 3
- group_weight: float32 [2048], P('var'), may hold values from 1 to 40
- copy_source: int32 [16, 16, 1024], P('var'), may hold values from 0 to 1023
- copy_slot: int32 [16, 16, 1024], P('var'), may hold values from -1 to 16383, as said below
Outputs:
- latent_new: float32 [4, 16, 16384], P(None, 'var')
- coef_change: float32 [4, 16384], P(None, 'var')
- residual_new: float32 [4, 16384], P(None, 'people')
Inputs may be any that keep to these rules, and one draw needn't show every extreme that they name: Each row is a trait's residual over people, scaled from 1 to 3 along the people. copy_slot[o, s, :] lists the slots (group-major among owner o's 128 groups of 128) filled from slab s; used entries come first and -1 marks the rest; the live entries of one owner are distinct; in each draw some slab fills an owner's whole list of 1024, for every owner, and one owner has all its lists full.
All inputs are finite; a program needn't handle non-finite values.
Results may differ from a plain program's by a relative error of at most 0.00012.
Values sent between devices are 32-bit elements; how exact they have to be, the bound alone decides.
A program may use at most 64 MiB of HBM per device.

v0:
```python
import math

import jax
import jax.numpy as jnp
from jax import lax
from jax.sharding import PartitionSpec as P

GSIZE = 128


step_length = 0.25


def select_columns(tables, indices):
    width = tables.shape[2]

    def select_one(inputs):
        table, column_ids = inputs
        onehot = (jnp.arange(width, dtype=jnp.int32)[:, None] == column_ids[None, :]).astype(
            jnp.float32
        )
        return jnp.dot(table, onehot, precision=lax.Precision.HIGHEST)

    return lax.map(select_one, (tables, indices))


def add_columns(values, indices, width):

    def add_one(inputs):
        block, column_ids = inputs
        onehot = (jnp.arange(width, dtype=jnp.int32)[:, None] == column_ids[None, :]).astype(
            jnp.float32
        )
        return lax.dot_general(
            block, onehot, (((1,), (1,)), ((), ())), precision=lax.Precision.HIGHEST
        )

    return lax.map(add_one, (values, indices))


def per_device(genotype, dosage_mean, residual, latent_old, group_weight, copy_source, copy_slot):
    var_count = lax.axis_size("var")
    var_width = genotype.shape[1]
    traits = residual.shape[0]
    copy_count = copy_source.shape[2]
    list_length = var_count * copy_count
    inverse_root = 1.0 / math.sqrt(residual.shape[1] * lax.axis_size("people"))
    dosages = genotype.astype(jnp.float32)
    partial_value = jnp.dot(residual, dosages, precision=lax.Precision.HIGHEST)
    products, residual_sums = lax.psum((partial_value, jnp.sum(residual, axis=1)), "people")
    correlation = (products - residual_sums[:, None] * dosage_mean[None, :]) * inverse_root
    landing_list = copy_slot[0]
    live_list = landing_list >= 0
    live_float = live_list.reshape(-1).astype(jnp.float32)
    wanted = lax.all_to_all(copy_source, "var", split_axis=1, concat_axis=0, tiled=True)[:, 0, :]
    tables = jnp.broadcast_to(correlation[None], (var_count, traits, var_width))
    outgoing = select_columns(tables, wanted)
    arrived = lax.all_to_all(outgoing, "var", split_axis=0, concat_axis=0, tiled=True)
    grad_copy = arrived.transpose(1, 0, 2).reshape(traits, list_length) * live_float[None, :]
    previous = latent_old.reshape(traits, list_length) * live_float[None, :]
    proposal = previous + step_length * grad_copy
    squares = jnp.sum(proposal * proposal, axis=0)
    group_count = group_weight.shape[0]
    group_list = jnp.where(live_list, landing_list // GSIZE, group_count).reshape(-1)
    membership = (jnp.arange(group_count, dtype=jnp.int32)[:, None] == group_list[None, :]).astype(
        jnp.float32
    )
    group_norm = jnp.sqrt(jnp.dot(membership, squares, precision=lax.Precision.HIGHEST))
    threshold = step_length * group_weight
    shrinkage = jnp.maximum(group_norm - threshold, 0.0) / jnp.maximum(group_norm, threshold)
    shrink_list = jnp.dot(shrinkage, membership, precision=lax.Precision.HIGHEST)
    latent_flat = proposal * shrink_list[None, :]
    changes = latent_flat - previous
    change_blocks = changes.reshape(traits, var_count, copy_count).transpose(1, 0, 2)
    returned = lax.all_to_all(change_blocks, "var", split_axis=0, concat_axis=0, tiled=True)
    coef_change = jnp.sum(add_columns(returned, wanted, var_width), axis=0)
    predicted_part = lax.dot_general(
        coef_change, dosages, (((1,), (1,)), ((), ())), precision=lax.Precision.HIGHEST
    )
    offset_part = jnp.dot(coef_change, dosage_mean, precision=lax.Precision.HIGHEST)
    predicted, offset_term = lax.psum((predicted_part, offset_part), "var")
    residual_new = residual - (predicted - offset_term[:, None]) * inverse_root
    return (latent_flat.reshape(latent_old.shape), coef_change, residual_new)


def solution(mesh):
    return jax.shard_map(
        per_device,
        mesh=mesh,
        in_specs=(
            P("people", "var"),
            P("var"),
            P(None, "people"),
            P(None, "var", None),
            P("var"),
            P("var", None, None),
            P("var", None, None),
        ),
        out_specs=(P(None, "var", None), P(None, "var"), P(None, "people")),
        check_vma=False,
    )
```

profile of v0, /device:TPU:2, one launch (start us, length us, event | category | flops | bytes accessed | tf_op | source)
XLA Modules:
  0.0 251.8 jit_solution(5222377517134760084)
XLA Ops:
  2.2 9.2 %all-to-all-start = ((s32[1,16,1024]{2,0,1:T(1,128)}), s32[1,16,1024]{2,0,1:T(1,128)S(1)}, u32[]{:S(2)}, u32[]{:S(2)}) async-start(s32[1,16,1024]{2,0,1:T(1,128)} %copy.18), calls=%async_computation | async-start | bytes 131072 | tf_op jit(solution)/shard_map/all_to_all | solution.py:55
  11.4 2.7 %fusion.20 = f32[4,1024]{1,0:T(4,128)S(1)} fusion(f32[4,512]{1,0:T(4,128)} %param.13, s32[512,1024]{1,0:T(8,128)} %param.11), kind=kOutput, calls=%fused_computation.25 | convolution fusion | flops 25690112 | bytes 2121728 | tf_op jit(solution)/shard_map/dot_general | solution.py:49
  14.3 96.6 %all-reduce = (f32[4,1024]{1,0:T(4,128)S(1)}, f32[4]{0:T(128)S(1)}) all-reduce(f32[4,1024]{1,0:T(4,128)S(1)} %fusion.20, f32[4]{0:T(128)S(1)} %reduce_sum.27), channel_id=1, replica_groups=mesh['people'=32,'var'=16] {'people'}, use_global_device_ids=true, to_apply=%region_0.0 | all-reduce | flops 4100 | bytes 32800 | tf_op jit(solution)/shard_map/psum | solution.py:50
  111.9 31.8 %while.20 = (s32[]{:T(128)}, f32[16,4,1024]{2,1,0:T(4,128)}, f32[16,4,1024]{2,1,0:T(4,128)S(1)}, s32[16,1024]{1,0:T(8,128)S(1)}, s32[]{:T(128)}) while((s32[]{:T(128)}, f32[16,4,1024]{2,1,0:T(4,128)}, f32[16,4,1024]{2,1,0:T(4,128)S(1)}, s32[16,1024]{1,0:T(8,128)S(1)}, s32[]{:T(128)}) %tuple.45), condition=%wide.region_4.5_spmd, body=%wide.region_3.4_spmd.sunk | while | flops 51380224 | bytes 46145 | solution.py:24
  111.9 2.0 fusion.50
  113.9 2.0 fusion.50
  115.9 2.0 fusion.50
  117.9 2.0 fusion.50
  119.9 2.0 fusion.50
  121.9 2.0 fusion.50
  123.8 2.0 fusion.50
  125.8 2.0 fusion.50
  127.8 2.0 fusion.50
  129.8 2.0 fusion.50
  131.8 2.0 fusion.50
  133.8 2.0 fusion.50
  139.8 2.0 fusion.50
  143.7 7.4 %all-to-all-start.1 = ((f32[16,4,1024]{2,1,0:T(4,128)}), f32[16,4,1024]{2,1,0:T(4,128)S(1)}, u32[]{:S(2)}, u32[]{:S(2)}) async-start(f32[16,4,1024]{2,1,0:T(4,128)} %get-tuple-element.47), calls=%async_computation.1 | async-start | bytes 524288 | tf_op jit(solution)/shard_map/all_to_all | solution.py:58
  151.2 7.3 %all-to-all-done.1 = f32[16,4,1024]{2,1,0:T(4,128)S(1)} async-done(((f32[16,4,1024]{2,1,0:T(4,128)}), f32[16,4,1024]{2,1,0:T(4,128)S(1)}, u32[]{:S(2)}, u32[]{:S(2)}) %all-to-all-start.1) | async-done | bytes 262176 | tf_op jit(solution)/shard_map/all_to_all | solution.py:58
  159.5 3.8 %fusion.23 = f32[128]{0:T(128)S(1)} fusion(f32[16384,1]{0,1:T(1,128)S(1)} %bitcast.87, s32[16384]{0:T(1024)S(1)} %fusion.28), kind=kOutput, calls=%fused_computation.29 | convolution fusion | flops 27262976 | bytes 131584 | tf_op jit(solution)/shard_map/dot_general | solution.py:68
  163.3 2.7 %fusion.14 = f32[1,16384]{1,0:T(1,128)S(1)} fusion(s32[16384]{0:T(1024)S(1)} %fusion.28, f32[128]{0:T(128)S(1)} %fusion.23, f32[128]{0:T(128)S(1)} %copy-done.6), kind=kOutput, calls=%fused_computation.19 | convolution fusion | flops 27263616 | bytes 132096 | tf_op jit(solution)/shard_map/dot_general | solution.py:71
  167.8 11.9 %all_to_all.19 = f32[16,4,1024]{2,1,0:T(4,128)S(1)} all-to-all(f32[16,4,1024]{2,1,0:T(4,128)S(1)} %copy.21), channel_id=1, replica_groups=mesh['people'=32,'var'=16] {'var'}, dimensions={0} | all-to-all | bytes 524288 | tf_op jit(solution)/shard_map/all_to_all | solution.py:75
  179.7 31.4 %while.21 = (s32[]{:T(128)}, f32[16,4,1024]{2,1,0:T(4,128)S(1)}, f32[16,4,1024]{2,1,0:T(4,128)S(1)}, s32[16,1024]{1,0:T(8,128)S(1)}, s32[]{:T(128)}) while((s32[]{:T(128)}, f32[16,4,1024]{2,1,0:T(4,128)S(1)}, f32[16,4,1024]{2,1,0:T(4,128)S(1)}, s32[16,1024]{1,0:T(8,128)S(1)}, s32[]{:T(128)}) %tuple.46), condition=%wide.region_7.8_spmd, body=%wide.region_6.7_spmd.sunk | while | flops 51380224 | bytes 46145 | solution.py:38
  213.2 37.9 %all-reduce.1 = (f32[4,512]{1,0:T(4,128)S(1)}, f32[4]{0:T(128)S(1)}) all-reduce(f32[4,512]{1,0:T(4,128)S(1)} %fusion.18, f32[4]{0:T(128)S(1)} %convolution_bitcast_fusion), channel_id=1, replica_groups=mesh['people'=32,'var'=16] {'var'}, use_global_device_ids=true, to_apply=%region_9.10 | all-reduce | flops 2052 | bytes 16416 | tf_op jit(solution)/shard_map/psum | solution.py:81
  (89 shorter events, 45.5 us)
Async XLA Ops:
  0.6 13.5 %copy-start.3 = (f32[4,512]{1,0:T(4,128)S(1)}, f32[4,512]{1,0:T(4,128)}, u32[]{:S(2)}) copy-start(f32[4,512]{1,0:T(4,128)} %param.13) | copy-start | bytes 24580
  0.6 13.7 %copy-start.2 = (s32[1,16,1024]{2,1,0:T(8,128)S(1)}, s32[1,16,1024]{2,1,0:T(8,128)}, u32[]{:S(2)}) copy-start(s32[1,16,1024]{2,1,0:T(8,128)} %param.17) | copy-start | bytes 196612
  0.7 110.3 %copy-start.5 = (f32[1024]{0:T(1024)S(1)}, f32[1024]{0:T(1024)}, u32[]{:S(2)}) copy-start(f32[1024]{0:T(1024)} %param.12) | copy-start | bytes 12292
  2.2 108.8 %all-to-all-start = ((s32[1,16,1024]{2,0,1:T(1,128)}), s32[1,16,1024]{2,0,1:T(1,128)S(1)}, u32[]{:S(2)}, u32[]{:S(2)}) async-start(s32[1,16,1024]{2,0,1:T(1,128)} %copy.18), calls=%async_computation | async-start | bytes 131072 | tf_op jit(solution)/shard_map/all_to_all | solution.py:55
  143.7 15.3 %copy-start.1 = (f32[4,1,16384]{2,1,0:T(1,128)S(1)}, f32[4,1,16384]{2,1,0:T(1,128)}, u32[]{:S(2)}) copy-start(f32[4,1,16384]{2,1,0:T(1,128)} %param.14) | copy-start | bytes 786436
  143.7 14.7 %all-to-all-start.1 = ((f32[16,4,1024]{2,1,0:T(4,128)}), f32[16,4,1024]{2,1,0:T(4,128)S(1)}, u32[]{:S(2)}, u32[]{:S(2)}) async-start(f32[16,4,1024]{2,1,0:T(4,128)} %get-tuple-element.47), calls=%async_computation.1 | async-start | bytes 524288 | tf_op jit(solution)/shard_map/all_to_all | solution.py:58
  151.2 12.1 %copy-start.6 = (f32[128]{0:T(128)S(1)}, f32[128]{0:T(128)}, u32[]{:S(2)}) copy-start(f32[128]{0:T(128)} %param.15) | copy-start | bytes 1540
  167.8 43.5 %copy-start = (s32[512,1024]{1,0:T(8,128)S(1)}, s32[512,1024]{1,0:T(8,128)}, u32[]{:S(2)}) copy-start(s32[512,1024]{1,0:T(8,128)} %param.11) | copy-start | bytes 6291460
  211.2 40.5 %copy-start.4 = (f32[4,1024]{1,0:T(4,128)}, f32[4,1024]{1,0:T(4,128)S(1)}, u32[]{:S(2)}) copy-start(f32[4,1024]{1,0:T(4,128)S(1)} %reduce_sum.29) | copy-start | bytes 49156
where the time goes:
time: 252 us
  blocking collectives  146 us (58%)
  matrix products  73.8 us (29%)
  starting transfers between devices  16.6 us (7%)
  waiting for transfers between devices  7.26 us (3%)
  local copies, waits for them, and re-layouts  3.71 us (1%)
  other arithmetic  2.94 us (1%)
    psum x1, blocking collectives, per_device(): lax.psum((partial_value, jnp.sum(residual, axis=1)), 'people')  96.6 us
    psum x1, blocking collectives, per_device(): predicted, offset_term = lax.psum((predicted_part, offset_part), 'var')  37.9 us
    dot_general x16, matrix products, select_one(): return jnp.dot(table, onehot, precision=lax.Precision.HIGHEST)  31.7 us
    dot_general x16, matrix products, add_one(): lax.dot_general(block, onehot, (((1,), (1,)), ((), ())), precision=lax.Pr...  31 us
    all_to_all x1, blocking collectives, per_device(): lax.all_to_all(change_blocks, 'var', split_axis=0, concat_axis=0, tiled=T...  11.9 us
    all_to_all x1, starting transfers between devices, per_device(): lax.all_to_all(copy_source, 'var', split_axis=1, concat_axis=0, tiled=True)  9.2 us
    all_to_all x1, starting transfers between devices, per_device(): lax.all_to_all(outgoing, 'var', split_axis=0, concat_axis=0, tiled=True)  7.36 us
    all_to_all x1, waiting for transfers between devices, per_device(): lax.all_to_all(outgoing, 'var', split_axis=0, concat_axis=0, tiled=True)  7.25 us
  transfers between devices with their start and end apart: 2, of which 1 were waited for; matrix products, arithmetic and copies ran while one was open for 1% of the time, Pallas kernels for 0%

commit v1 on v0

v1 whole, which is shorter than its diff:
```python
import functools
import math

import jax
import jax.numpy as jnp
from jax import lax
from jax.experimental import pallas as pl
from jax.experimental.pallas import tpu as pltpu
from jax.sharding import PartitionSpec as P

MESH = pl.DeviceIdType.MESH
F32 = jnp.float32
BF16 = jnp.bfloat16
STEP = 0.25
LIST_ROWS = 56


def split3(a):
    first = a.astype(BF16).astype(F32)
    rest = a - first
    second = rest.astype(BF16).astype(F32)
    return first, second, rest - second


def kernel(n_people, n_var, inverse_root,
           geno, mean_h, res_h, lat_h, weight_h, source_h, slot_h,
           lat_out, coef_out, res_out,
           gi, gb, mean, res, lat, weight, source, slot,
           snd, rcv, pc, spc, zland, corr, tables, member, lows,
           prev, prop, squares, gland, thr, amat, latbuf, latland,
           cpart, csib, coef, pland, pbuf,
           in_sems, send_sems, recv_sems, out_sems):
    p, v = lax.axis_index("people"), lax.axis_index("var")
    n_z = n_people // 2
    core = lax.rem(p, 2)
    z = p // 2
    half = n_var // 2
    active = (v // half) == core
    sibling = {"people": p + 1 - 2 * core, "var": v}
    z_order = sorted(range(1, n_z), key=lambda d: -min(d, n_z - d))
    z_peers = [{"people": lax.rem(p + 2 * d, n_people), "var": v} for d in z_order]
    var_peers = [{"people": p, "var": lax.rem(v + d, n_var)} for d in range(1, n_var)]

    def local(src, dst, sem):
        copy = pltpu.make_async_copy(src, dst, sem)
        copy.start()
        return copy

    def remote(src, dst, k, device):
        copy = pltpu.make_async_remote_copy(src_ref=src, dst_ref=dst, send_sem=send_sems.at[k], recv_sem=recv_sems.at[k],
                                            device_id=device, device_id_type=MESH)
        copy.start()

    def drain(ref, sem):
        pltpu.make_async_copy(ref, ref, sem).wait()

    barrier = pltpu.get_barrier_semaphore()
    for device in z_peers + var_peers + [sibling]:
        pl.semaphore_signal(barrier, inc=1, device_id=device, device_id_type=MESH)

    people_dev = gi.shape[0]
    chunk = people_dev // 4
    small = [local(res_h, res, in_sems.at[4]), local(mean_h, mean, in_sems.at[5])]
    big = [local(geno.at[pl.ds(chunk * k, chunk), :], gi.at[pl.ds(chunk * k, chunk), :], in_sems.at[k]) for k in range(4)]
    lists = [local(lat_h, lat, in_sems.at[6]), local(weight_h, weight, in_sems.at[7]),
             local(source_h, source, in_sems.at[8]), local(slot_h, slot, in_sems.at[9])]

    for copy in small:
        copy.wait()
    residual = res[...]
    sums = jnp.sum(residual, axis=1, keepdims=True)
    parts = jnp.concatenate(split3(residual), axis=0).astype(BF16)
    total = None
    for k in range(4):
        big[k].wait()
        rows = pl.ds(chunk * k, chunk)
        block = gi[rows, :].astype(F32).astype(BF16)
        gb[rows, :] = block
        term = jnp.dot(parts[:, chunk * k:chunk * (k + 1)], block, preferred_element_type=F32)
        total = term if total is None else total + term
    products = total[8:12] + total[4:8] + total[0:4] - sums * mean[...]
    for h in range(8):
        pc[pl.ds(h, 4, stride=8), :] = products[:, 128 * h:128 * (h + 1)]

    for copy in lists:
        copy.wait()
    for i in range(n_var // 8):
        for j in range(8):
            block = pl.ds(8 * i * LIST_ROWS + 32 + j, 8, stride=LIST_ROWS)
            snd[block, :] = source[8 * i:8 * i + 8, 128 * j:128 * (j + 1)].astype(F32)
            block = pl.ds(8 * i * LIST_ROWS + 40 + j, 8, stride=LIST_ROWS)
            snd[block, :] = slot[8 * i:8 * i + 8, 128 * j:128 * (j + 1)].astype(F32)
    for s in range(n_var):
        for t in range(4):
            snd[LIST_ROWS * s + 8 * t:LIST_ROWS * s + 8 * t + 8, :] = lat[t, 8 * s:8 * s + 8, :]
        snd[LIST_ROWS * s + 48:LIST_ROWS * s + 56, :] = jnp.broadcast_to(weight[...], (8, 128))

    pl.semaphore_wait(barrier, n_z - 1 + n_var - 1 + 1)

    remote(pc, spc, 0, sibling)
    drain(pc, recv_sems.at[0])
    zland[z] = pc[...] + spc[...]
    for device in z_peers:
        remote(zland.at[z], zland.at[z], 1, device)

    def slab_rows(s):
        return pl.ds(pl.multiple_of(s * LIST_ROWS, 8), LIST_ROWS)

    mine = lax.rem(v, half)

    @pl.when(active)
    def _():
        for d in range(1, n_var):
            other = lax.rem(v + d, n_var)
            remote(snd.at[slab_rows(other), :], rcv.at[mine], 2, {"people": p, "var": other})
        rcv[mine] = snd[slab_rows(v), :]
        drain(rcv.at[pl.ds(0, half - 1)], recv_sems.at[2])

    @pl.when(jnp.logical_not(active))
    def _():
        drain(rcv, recv_sems.at[2])

    rows_iota = lax.broadcasted_iota(jnp.int32, (128, 128), 0)

    def prepare(o, carry):
        sources = rcv[o, 32:40, :].astype(jnp.int32)
        slots = rcv[o, 40:48, :].astype(jnp.int32)
        live = slots >= 0
        group = jnp.where(live, lax.shift_right_arithmetic(slots, 7), -1)
        low = lax.bitwise_and(sources, 127)
        for j in range(8):
            member[o, :, 128 * j:128 * (j + 1)] = jnp.where(rows_iota == group[j:j + 1, :], 1.0, 0.0).astype(BF16)
            lows[o, :, 128 * j:128 * (j + 1)] = jnp.where(rows_iota == low[j:j + 1, :], 1.0, 0.0).astype(BF16)
        for t in range(4):
            prev[o, 8 * t:8 * t + 8, :] = jnp.where(live, rcv[o, 8 * t:8 * t + 8, :], 0.0)
        thr[pl.ds(o, 1), :] = STEP * rcv[o, 48:49, :]
        return carry

    lax.fori_loop(0, half, prepare, 0)

    drain(zland.at[pl.ds(0, n_z - 1)], recv_sems.at[1])
    summed = zland[0]
    for k in range(1, n_z):
        summed = summed + zland[k]
    corr[...] = summed * inverse_root
    for t in range(4):
        for h in range(8):
            tables[8 * t + h] = jnp.broadcast_to(corr[8 * t + h:8 * t + h + 1, :], (8, 128))

    def propose(o, carry):
        sources = rcv[o, 32:40, :].astype(jnp.int32)
        live = rcv[o, 40:48, :] >= 0.0
        high = lax.shift_right_arithmetic(sources, 7)
        low = lax.bitwise_and(sources, 127)
        total = jnp.zeros((8, 128), F32)
        for t in range(4):
            picked = jnp.zeros((8, 128), F32)
            for h in range(8):
                picked = jnp.where(high == h, jnp.take_along_axis(tables[8 * t + h], low, axis=1), picked)
            value = prev[o, 8 * t:8 * t + 8, :] + STEP * jnp.where(live, picked, 0.0)
            prop[o, 8 * t:8 * t + 8, :] = value
            total = total + value * value
        squares[pl.ds(pl.multiple_of(8 * o, 8), 8), :] = total
        return carry

    lax.fori_loop(0, half, propose, 0)
    by_owner = jnp.concatenate([squares[pl.ds(j, half, stride=8), :] for j in range(8)], axis=1)
    stacked = jnp.concatenate(split3(by_owner), axis=0).astype(BF16)
    owner_iota = lax.broadcasted_iota(jnp.int32, (half, 128), 0)
    partial = jnp.zeros((half, 128), F32)
    for o in range(half):
        one = lax.dot_general(stacked, member[o], (((1,), (1,)), ((), ())), preferred_element_type=F32)
        one = one[2 * half:3 * half] + one[half:2 * half] + one[0:half]
        partial = jnp.where(owner_iota == o, one, partial)
    gland[v] = partial
    for device in var_peers:
        remote(gland.at[v], gland.at[v], 3, device)
    drain(gland.at[pl.ds(0, n_var - 1)], recv_sems.at[3])
    norm = gland[0]
    for k in range(1, n_var):
        norm = norm + gland[k]
    norm = jnp.sqrt(norm)
    threshold = thr[...]
    shrink = jnp.maximum(norm - threshold, 0.0) / jnp.maximum(norm, threshold)
    squares[0:half, :] = shrink

    hi_iota = lax.broadcasted_iota(jnp.int32, (8, 128), 0)

    def change(o, carry):
        slots = rcv[o, 40:48, :].astype(jnp.int32)
        live = slots >= 0
        group = jnp.where(live, lax.shift_right_arithmetic(slots, 7), 0)
        high = lax.shift_right_arithmetic(rcv[o, 32:40, :].astype(jnp.int32), 7)
        table = jnp.broadcast_to(squares[pl.ds(o, 1), :], (8, 128))
        factor = jnp.where(live, jnp.take_along_axis(table, group, axis=1), 0.0)
        deltas = []
        for t in range(4):
            fresh = prop[o, 8 * t:8 * t + 8, :] * factor
            latbuf[o, t] = fresh
            deltas.append(fresh - prev[o, 8 * t:8 * t + 8, :])
        for j in range(8):
            mask = hi_iota == high[j:j + 1, :]
            block = jnp.concatenate([jnp.where(mask, deltas[t][j:j + 1, :], 0.0) for t in range(4)], axis=0)
            first = block.astype(BF16)
            second = (block - first.astype(F32)).astype(BF16)
            amat[o, 0:32, 128 * j:128 * (j + 1)] = first
            amat[o, 32:64, 128 * j:128 * (j + 1)] = second
        return carry

    lax.fori_loop(0, half, change, 0)
    acc = jnp.zeros((64, 128), F32)
    for o in range(half):
        acc = acc + lax.dot_general(amat[o], lows[o], (((1,), (1,)), ((), ())), preferred_element_type=F32)
    cpart[...] = acc[32:64] + acc[0:32]
    remote(cpart, csib, 4, sibling)

    slab_place = pl.ds(pl.multiple_of(8 * v, 8), 8)
    for o in range(half):
        owner = core * half + o

        @pl.when(owner != v)
        def _():
            remote(latbuf.at[o], latland.at[:, slab_place, :], 5, {"people": p, "var": owner})

    @pl.when(active)
    def _():
        latland[:, slab_place, :] = latbuf[mine]

    drain(cpart, recv_sems.at[4])
    coef[...] = cpart[...] + csib[...]
    wide = jnp.concatenate([coef[pl.ds(h, 4, stride=8), :] for h in range(8)], axis=1)
    coef_out[...] = wide
    offset = jnp.sum(wide * mean[...], axis=1, keepdims=True)
    pieces = jnp.concatenate(split3(wide), axis=0).astype(BF16)
    fitted = lax.dot_general(pieces, gb[...], (((1,), (1,)), ((), ())), preferred_element_type=F32)
    fitted = fitted[8:12] + fitted[4:8] + fitted[0:4] - offset
    lanes = people_dev // 128
    for k in range(lanes):
        pbuf[4 * k:4 * k + 4, :] = fitted[:, 128 * k:128 * (k + 1)]
    pland[v] = pbuf[...]
    for device in var_peers:
        remote(pland.at[v], pland.at[v], 6, device)

    @pl.when(active)
    def _():
        drain(latland.at[:, pl.ds(0, 8 * (n_var - 1)), :], recv_sems.at[5])
        remote(latland, latland, 7, sibling)

    @pl.when(jnp.logical_not(active))
    def _():
        drain(latland, recv_sems.at[7])

    local(latland, lat_out, out_sems.at[0])

    drain(pland.at[pl.ds(0, n_var - 1)], recv_sems.at[6])
    predicted = pland[0]
    for k in range(1, n_var):
        predicted = predicted + pland[k]
    for k in range(lanes):
        res_out[:, 128 * k:128 * (k + 1)] = residual[:, 128 * k:128 * (k + 1)] - predicted[4 * k:4 * k + 4, :] * inverse_root

    drain(lat_out, out_sems.at[0])
    drain(pc, send_sems.at[0])
    drain(zland.at[pl.ds(0, n_z - 1)], send_sems.at[1])
    drain(gland.at[pl.ds(0, n_var - 1)], send_sems.at[3])
    drain(cpart, send_sems.at[4])
    drain(pland.at[pl.ds(0, n_var - 1)], send_sems.at[6])

    @pl.when(active)
    def _():
        drain(snd.at[pl.ds(0, LIST_ROWS * (n_var - 1)), :], send_sems.at[2])
        drain(latbuf.at[pl.ds(0, half - 1)], send_sems.at[5])
        drain(latland, send_sems.at[7])

    @pl.when(jnp.logical_not(active))
    def _():
        drain(latbuf, send_sems.at[5])


def per_device(n_people, n_var, genotype, dosage_mean, residual, latent_old, group_weight, copy_source, copy_slot):
    people_dev, var_dev = genotype.shape
    traits = residual.shape[0]
    inverse_root = 1.0 / math.sqrt(people_dev * n_people)
    half = n_var // 2
    n_z = n_people // 2
    list_rows = n_var * var_dev // 128
    vmem = pl.BlockSpec(memory_space=pltpu.VMEM)
    hbm = pl.BlockSpec(memory_space=pl.ANY)
    lat, coef, res = pl.pallas_call(
        functools.partial(kernel, n_people, n_var, inverse_root),
        out_shape=(
            jax.ShapeDtypeStruct((traits, list_rows, 128), F32),
            jax.ShapeDtypeStruct((traits, var_dev), F32),
            jax.ShapeDtypeStruct((traits, people_dev), F32),
        ),
        in_specs=[hbm] * 7,
        out_specs=(hbm, vmem, vmem),
        scratch_shapes=[
            pltpu.VMEM((people_dev, var_dev), jnp.int32),
            pltpu.VMEM((people_dev, var_dev), BF16),
            pltpu.VMEM((1, var_dev), F32),
            pltpu.VMEM((traits, people_dev), F32),
            pltpu.VMEM((traits, list_rows, 128), F32),
            pltpu.VMEM((1, 128), F32),
            pltpu.VMEM((n_var, 1024), jnp.int32),
            pltpu.VMEM((n_var, 1024), jnp.int32),
            pltpu.VMEM((n_var * LIST_ROWS, 128), F32),
            pltpu.VMEM((half, LIST_ROWS, 128), F32),
            pltpu.VMEM((32, 128), F32),
            pltpu.VMEM((32, 128), F32),
            pltpu.VMEM((n_z, 32, 128), F32),
            pltpu.VMEM((32, 128), F32),
            pltpu.VMEM((32, 8, 128), F32),
            pltpu.VMEM((half, 128, 1024), BF16),
            pltpu.VMEM((half, 128, 1024), BF16),
            pltpu.VMEM((half, 32, 128), F32),
            pltpu.VMEM((half, 32, 128), F32),
            pltpu.VMEM((half * 8, 128), F32),
            pltpu.VMEM((n_var, half, 128), F32),
            pltpu.VMEM((half, 128), F32),
            pltpu.VMEM((half, 64, 1024), BF16),
            pltpu.VMEM((half, traits, 8, 128), F32),
            pltpu.VMEM((traits, list_rows, 128), F32),
            pltpu.VMEM((32, 128), F32),
            pltpu.VMEM((32, 128), F32),
            pltpu.VMEM((32, 128), F32),
            pltpu.VMEM((n_var, people_dev // 32, 128), F32),
            pltpu.VMEM((people_dev // 32, 128), F32),
            pltpu.SemaphoreType.DMA((10,)),
            pltpu.SemaphoreType.DMA((8,)),
            pltpu.SemaphoreType.DMA((8,)),
            pltpu.SemaphoreType.DMA((1,)),
        ],
        compiler_params=pltpu.CompilerParams(collective_id=0, has_side_effects=True, vmem_limit_bytes=62 * 2**20),
    )(
        genotype,
        dosage_mean.reshape(1, var_dev),
        residual,
        latent_old.reshape(traits, list_rows, 128),
        group_weight.reshape(1, 128),
        copy_source[0],
        copy_slot[0],
    )
    return lat.reshape(latent_old.shape), coef, res


def solution(mesh):
    return jax.shard_map(
        functools.partial(per_device, mesh.shape["people"], mesh.shape["var"]),
        mesh=mesh,
        in_specs=(
            P("people", "var"),
            P("var"),
            P(None, "people"),
            P(None, "var", None),
            P("var"),
            P("var", None, None),
            P("var", None, None),
        ),
        out_specs=(P(None, "var", None), P(None, "var"), P(None, "people")),
        check_vma=False,
    )
```

time: 252 us -> 53.3 us (0.21)
  the two profiles are of different devices: /device:TPU:2 before, /device:TPU:1 now
where the time goes in v1:
time: 53.3 us; the launch traced here: 52.9 us
  Pallas kernels  48 us (90%)
  local copies, waits for them, and re-layouts  4.29 us (8%)
  between operations  0.64 us (1%)
    pallas_call x1, Pallas kernels, per_device(): pl.pallas_call(functools.partial(kernel, n_people, n_var, inverse_root),...  48 us
    unnamed x3, local copies, waits for them, and re-layouts  4.29 us

profile of v1, /device:TPU:1, one launch (start us, length us, event | category | flops | bytes accessed | tf_op | source)
XLA Modules:
  0.0 52.9 jit_solution(12148274114471599359)
XLA Ops:
  0.6 48.0 %shard_map.94 = (f32[4,128,128]{2,1,0:T(8,128)}, f32[4,1024]{1,0:T(4,128)}, f32[4,512]{1,0:T(4,128)}) custom-call(s32[512,1024]{1,0:T(8,128)} %geno.1, f32[1,1024]{1,0:T(1,128)} %bitcast.10, f32[4,512]{1,0:T(4,128)} %res_h.1, f32[4,128,128]{2,1,0:T(8,128)} %bitcast.7, f32[1,128]{1,0:T(1,128)} %bitcast.11, s32[16,1024]{1,0:T(8,128)} %bitcast.8, ...), custom_call_target="tpu_custom_call" | custom-call | tf_op jit(solution)/shard_map/pallas_call | solution.py:289
  48.6 1.7 %copy.14 = f32[4,1,16384]{2,1,0:T(1,128)} copy(f32[4,1,16384]{2,1,0:T(1,128)} %bitcast.6) | data formatting | bytes 524288
  50.3 1.3 %copy.15 = f32[4,1024]{1,0:T(4,128)} copy(f32[4,1024]{1,0:T(4,128)} %get-tuple-element.16) | data formatting | bytes 32768
  51.6 1.3 %copy.16 = f32[4,512]{1,0:T(4,128)} copy(f32[4,512]{1,0:T(4,128)} %get-tuple-element.17) | data formatting | bytes 16384

commit v2 on v1

--- a/solution.py
+++ b/solution.py
@@ -26,10 +26,10 @@
            geno, mean_h, res_h, lat_h, weight_h, source_h, slot_h,
            lat_out, coef_out, res_out,
            gi, gb, mean, res, lat, weight, source, slot,
-           snd, rcv, pc, spc, zland, corr, tables, member, lows,
-           prev, prop, squares, gland, thr, amat, latbuf, latland,
+           snd, rcv, pc, win, wsum, halves, corr, tables, member, lows,
+           highs, prev, prop, squares, gland, thr, amat, latbuf, latland,
            cpart, csib, coef, pland, pbuf,
-           in_sems, send_sems, recv_sems, out_sems):
+           in_sems, send_sems, recv_sems):
     p, v = lax.axis_index("people"), lax.axis_index("var")
     n_z = n_people // 2
     core = lax.rem(p, 2)
@@ -37,8 +37,13 @@
     half = n_var // 2
     active = (v // half) == core
     sibling = {"people": p + 1 - 2 * core, "var": v}
-    z_order = sorted(range(1, n_z), key=lambda d: -min(d, n_z - d))
-    z_peers = [{"people": lax.rem(p + 2 * d, n_people), "var": v} for d in z_order]
+    reach = n_z // 4
+
+    def along(d, other=False):
+        return {"people": 2 * lax.rem(z + d + n_z, n_z) + (1 - core if other else core), "var": v}
+
+    near = sorted((d for d in range(-reach, reach + 1) if d != 0), key=lambda d: -abs(d))
+    z_peers = [along(d) for d in near] + [along(reach, True), along(-reach, True)]
     var_peers = [{"people": p, "var": lax.rem(v + d, n_var)} for d in range(1, n_var)]
 
     def local(src, dst, sem):
@@ -95,13 +100,12 @@
             snd[LIST_ROWS * s + 8 * t:LIST_ROWS * s + 8 * t + 8, :] = lat[t, 8 * s:8 * s + 8, :]
         snd[LIST_ROWS * s + 48:LIST_ROWS * s + 56, :] = jnp.broadcast_to(weight[...], (8, 128))
 
-    pl.semaphore_wait(barrier, n_z - 1 + n_var - 1 + 1)
-
-    remote(pc, spc, 0, sibling)
-    drain(pc, recv_sems.at[0])
-    zland[z] = pc[...] + spc[...]
-    for device in z_peers:
-        remote(zland.at[z], zland.at[z], 1, device)
+    pl.semaphore_wait(barrier, len(z_peers) + len(var_peers) + 1)
+
+    win[reach] = pc[...]
+    for d in near:
+        if d < reach:
+            remote(pc, win.at[reach + d], 1, along(-d))
 
     def slab_rows(s):
         return pl.ds(pl.multiple_of(s * LIST_ROWS, 8), LIST_ROWS)
@@ -114,6 +118,18 @@
             other = lax.rem(v + d, n_var)
             remote(snd.at[slab_rows(other), :], rcv.at[mine], 2, {"people": p, "var": other})
         rcv[mine] = snd[slab_rows(v), :]
+
+    drain(win.at[pl.ds(0, 2 * reach - 1)], recv_sems.at[1])
+    summed = win[0]
+    for k in range(1, 2 * reach):
+        summed = summed + win[k]
+    wsum[...] = summed
+    for k, d in enumerate((-reach, reach)):
+        for other in (False, True):
+            remote(wsum, halves.at[2 * core + k], 0, along(d, other))
+
+    @pl.when(active)
+    def _():
         drain(rcv.at[pl.ds(0, half - 1)], recv_sems.at[2])
 
     @pl.when(jnp.logical_not(active))
@@ -121,6 +137,8 @@
         drain(rcv, recv_sems.at[2])
 
     rows_iota = lax.broadcasted_iota(jnp.int32, (128, 128), 0)
+    lanes_iota = lax.broadcasted_iota(jnp.int32, (128, 128), 1)
+    hi_iota = lax.broadcasted_iota(jnp.int32, (8, 128), 0)
 
     def prepare(o, carry):
         sources = rcv[o, 32:40, :].astype(jnp.int32)
@@ -128,9 +146,14 @@
         live = slots >= 0
         group = jnp.where(live, lax.shift_right_arithmetic(slots, 7), -1)
         low = lax.bitwise_and(sources, 127)
+        high = lax.shift_right_arithmetic(sources, 7)
+        low_columns = low.T
         for j in range(8):
-            member[o, :, 128 * j:128 * (j + 1)] = jnp.where(rows_iota == group[j:j + 1, :], 1.0, 0.0).astype(BF16)
-            lows[o, :, 128 * j:128 * (j + 1)] = jnp.where(rows_iota == low[j:j + 1, :], 1.0, 0.0).astype(BF16)
+            rows = pl.ds(pl.multiple_of(128 * o, 128), 128)
+            member[rows, 128 * j:128 * (j + 1)] = jnp.where(rows_iota == group[j:j + 1, :], 1.0, 0.0).astype(BF16)
+            rows = pl.ds(pl.multiple_of(1024 * o + 128 * j, 128), 128)
+            lows[rows, :] = jnp.where(lanes_iota == low_columns[:, j:j + 1], 1.0, 0.0).astype(BF16)
+            highs[8 * o + j] = jnp.where(hi_iota == high[j:j + 1, :], 1.0, 0.0)
         for t in range(4):
             prev[o, 8 * t:8 * t + 8, :] = jnp.where(live, rcv[o, 8 * t:8 * t + 8, :], 0.0)
         thr[pl.ds(o, 1), :] = STEP * rcv[o, 48:49, :]
@@ -138,16 +161,13 @@
 
     lax.fori_loop(0, half, prepare, 0)
 
-    drain(zland.at[pl.ds(0, n_z - 1)], recv_sems.at[1])
-    summed = zland[0]
-    for k in range(1, n_z):
-        summed = summed + zland[k]
-    corr[...] = summed * inverse_root
+    drain(halves, recv_sems.at[0])
+    corr[...] = ((halves[0] + halves[1]) + (halves[2] + halves[3])) * inverse_root
     for t in range(4):
         for h in range(8):
             tables[8 * t + h] = jnp.broadcast_to(corr[8 * t + h:8 * t + h + 1, :], (8, 128))
 
-    def propose(o, carry):
+    for o in range(half):
         sources = rcv[o, 32:40, :].astype(jnp.int32)
         live = rcv[o, 40:48, :] >= 0.0
         high = lax.shift_right_arithmetic(sources, 7)
@@ -160,18 +180,15 @@
             value = prev[o, 8 * t:8 * t + 8, :] + STEP * jnp.where(live, picked, 0.0)
             prop[o, 8 * t:8 * t + 8, :] = value
             total = total + value * value
-        squares[pl.ds(pl.multiple_of(8 * o, 8), 8), :] = total
-        return carry
-
-    lax.fori_loop(0, half, propose, 0)
+        squares[8 * o:8 * o + 8, :] = total
     by_owner = jnp.concatenate([squares[pl.ds(j, half, stride=8), :] for j in range(8)], axis=1)
     stacked = jnp.concatenate(split3(by_owner), axis=0).astype(BF16)
     owner_iota = lax.broadcasted_iota(jnp.int32, (half, 128), 0)
-    partial = jnp.zeros((half, 128), F32)
-    for o in range(half):
-        one = lax.dot_general(stacked, member[o], (((1,), (1,)), ((), ())), preferred_element_type=F32)
-        one = one[2 * half:3 * half] + one[half:2 * half] + one[0:half]
-        partial = jnp.where(owner_iota == o, one, partial)
+    wide = lax.dot_general(stacked, member[...], (((1,), (1,)), ((), ())), preferred_element_type=F32)
+    wide = wide[2 * half:3 * half] + wide[half:2 * half] + wide[0:half]
+    partial = wide[:, 0:128]
+    for o in range(1, half):
+        partial = jnp.where(owner_iota == o, wide[:, 128 * o:128 * (o + 1)], partial)
     gland[v] = partial
     for device in var_peers:
         remote(gland.at[v], gland.at[v], 3, device)
@@ -184,37 +201,27 @@
     shrink = jnp.maximum(norm - threshold, 0.0) / jnp.maximum(norm, threshold)
     squares[0:half, :] = shrink
 
-    hi_iota = lax.broadcasted_iota(jnp.int32, (8, 128), 0)
-
-    def change(o, carry):
+    slab_place = pl.ds(pl.multiple_of(8 * v, 8), 8)
+    for o in range(half):
         slots = rcv[o, 40:48, :].astype(jnp.int32)
         live = slots >= 0
         group = jnp.where(live, lax.shift_right_arithmetic(slots, 7), 0)
-        high = lax.shift_right_arithmetic(rcv[o, 32:40, :].astype(jnp.int32), 7)
-        table = jnp.broadcast_to(squares[pl.ds(o, 1), :], (8, 128))
+        table = jnp.broadcast_to(squares[o:o + 1, :], (8, 128))
         factor = jnp.where(live, jnp.take_along_axis(table, group, axis=1), 0.0)
-        deltas = []
+        firsts, seconds = [], []
         for t in range(4):
             fresh = prop[o, 8 * t:8 * t + 8, :] * factor
             latbuf[o, t] = fresh
-            deltas.append(fresh - prev[o, 8 * t:8 * t + 8, :])
+            delta = fresh - prev[o, 8 * t:8 * t + 8, :]
+            first = delta.astype(BF16).astype(F32)
+            firsts.append(first)
+            seconds.append(delta - first)
         for j in range(8):
-            mask = hi_iota == high[j:j + 1, :]
-            block = jnp.concatenate([jnp.where(mask, deltas[t][j:j + 1, :], 0.0) for t in range(4)], axis=0)
-            first = block.astype(BF16)
-            second = (block - first.astype(F32)).astype(BF16)
-            amat[o, 0:32, 128 * j:128 * (j + 1)] = first
-            amat[o, 32:64, 128 * j:128 * (j + 1)] = second
-        return carry
-
-    lax.fori_loop(0, half, change, 0)
-    acc = jnp.zeros((64, 128), F32)
-    for o in range(half):
-        acc = acc + lax.dot_general(amat[o], lows[o], (((1,), (1,)), ((), ())), preferred_element_type=F32)
-    cpart[...] = acc[32:64] + acc[0:32]
-    remote(cpart, csib, 4, sibling)
-
-    slab_place = pl.ds(pl.multiple_of(8 * v, 8), 8)
+            mask = highs[8 * o + j]
+            for k, terms in enumerate((firsts, seconds)):
+                block = jnp.concatenate([mask * term[j:j + 1, :] for term in terms], axis=0)
+                amat[32 * k:32 * k + 32, 1024 * o + 128 * j:1024 * o + 128 * (j + 1)] = block.astype(BF16)
+
     for o in range(half):
         owner = core * half + o
 
@@ -225,6 +232,10 @@
     @pl.when(active)
     def _():
         latland[:, slab_place, :] = latbuf[mine]
+
+    acc = jnp.dot(amat[...], lows[...], preferred_element_type=F32)
+    cpart[...] = acc[32:64] + acc[0:32]
+    remote(cpart, csib, 4, sibling)
 
     drain(cpart, recv_sems.at[4])
     coef[...] = cpart[...] + csib[...]
@@ -250,7 +261,7 @@
     def _():
         drain(latland, recv_sems.at[7])
 
-    local(latland, lat_out, out_sems.at[0])
+    lat_out[...] = latland[...]
 
     drain(pland.at[pl.ds(0, n_var - 1)], recv_sems.at[6])
     predicted = pland[0]
@@ -259,9 +270,8 @@
     for k in range(lanes):
         res_out[:, 128 * k:128 * (k + 1)] = residual[:, 128 * k:128 * (k + 1)] - predicted[4 * k:4 * k + 4, :] * inverse_root
 
-    drain(lat_out, out_sems.at[0])
-    drain(pc, send_sems.at[0])
-    drain(zland.at[pl.ds(0, n_z - 1)], send_sems.at[1])
+    drain(halves, send_sems.at[0])
+    drain(win.at[pl.ds(0, 2 * reach - 1)], send_sems.at[1])
     drain(gland.at[pl.ds(0, n_var - 1)], send_sems.at[3])
     drain(cpart, send_sems.at[4])
     drain(pland.at[pl.ds(0, n_var - 1)], send_sems.at[6])
@@ -275,6 +285,15 @@
     @pl.when(jnp.logical_not(active))
     def _():
         drain(latbuf, send_sems.at[5])
+
+
+def hand_out(lat, coef, res, lat_out, coef_out, res_out, sems):
+    copies = [pltpu.make_async_copy(src, dst, sems.at[k])
+              for k, (src, dst) in enumerate(((lat, lat_out), (coef, coef_out), (res, res_out)))]
+    for copy in copies:
+        copy.start()
+    for copy in copies:
+        copy.wait()
 
 
 def per_device(n_people, n_var, genotype, dosage_mean, residual, latent_old, group_weight, copy_source, copy_slot):
@@ -285,16 +304,13 @@
     n_z = n_people // 2
     list_rows = n_var * var_dev // 128
     vmem = pl.BlockSpec(memory_space=pltpu.VMEM)
-    hbm = pl.BlockSpec(memory_space=pl.ANY)
-    lat, coef, res = pl.pallas_call(
+    hbm = pl.BlockSpec(memory_space=pltpu.HBM)
+    shapes = ((traits, list_rows, 128), (traits, var_dev), (traits, people_dev))
+    held = pl.pallas_call(
         functools.partial(kernel, n_people, n_var, inverse_root),
-        out_shape=(
-            jax.ShapeDtypeStruct((traits, list_rows, 128), F32),
-            jax.ShapeDtypeStruct((traits, var_dev), F32),
-            jax.ShapeDtypeStruct((traits, people_dev), F32),
-        ),
+        out_shape=tuple(pltpu.VMEM(shape, F32) for shape in shapes),
         in_specs=[hbm] * 7,
-        out_specs=(hbm, vmem, vmem),
+        out_specs=(vmem,) * 3,
         scratch_shapes=[
             pltpu.VMEM((people_dev, var_dev), jnp.int32),
             pltpu.VMEM((people_dev, var_dev), BF16),
@@ -307,18 +323,20 @@
             pltpu.VMEM((n_var * LIST_ROWS, 128), F32),
             pltpu.VMEM((half, LIST_ROWS, 128), F32),
             pltpu.VMEM((32, 128), F32),
-            pltpu.VMEM((32, 128), F32),
-            pltpu.VMEM((n_z, 32, 128), F32),
+            pltpu.VMEM((n_z // 2, 32, 128), F32),
+            pltpu.VMEM((32, 128), F32),
+            pltpu.VMEM((4, 32, 128), F32),
             pltpu.VMEM((32, 128), F32),
             pltpu.VMEM((32, 8, 128), F32),
-            pltpu.VMEM((half, 128, 1024), BF16),
-            pltpu.VMEM((half, 128, 1024), BF16),
+            pltpu.VMEM((half * 128, 1024), BF16),
+            pltpu.VMEM((half * 1024, 128), BF16),
+            pltpu.VMEM((half * 8, 8, 128), F32),
             pltpu.VMEM((half, 32, 128), F32),
             pltpu.VMEM((half, 32, 128), F32),
             pltpu.VMEM((half * 8, 128), F32),
             pltpu.VMEM((n_var, half, 128), F32),
             pltpu.VMEM((half, 128), F32),
-            pltpu.VMEM((half, 64, 1024), BF16),
+            pltpu.VMEM((64, half * 1024), BF16),
             pltpu.VMEM((half, traits, 8, 128), F32),
             pltpu.VMEM((traits, list_rows, 128), F32),
             pltpu.VMEM((32, 128), F32),
@@ -329,10 +347,9 @@
             pltpu.SemaphoreType.DMA((10,)),
             pltpu.SemaphoreType.DMA((8,)),
             pltpu.SemaphoreType.DMA((8,)),
-            pltpu.SemaphoreType.DMA((1,)),
         ],
-        compiler_params=pltpu.CompilerParams(collective_id=0, has_side_effects=True, vmem_limit_bytes=62 * 2**20),
-    )(
+        compiler_params=pltpu.CompilerParams(collective_id=0, has_side_effects=True, vmem_limit_bytes=32 * 2**20),
+    )(*(pltpu.with_memory_space_constraint(x, pltpu.HBM) for x in (
         genotype,
         dosage_mean.reshape(1, var_dev),
         residual,
@@ -340,7 +357,14 @@
         group_weight.reshape(1, 128),
         copy_source[0],
         copy_slot[0],
-    )
+    )))
+    lat, coef, res = pl.pallas_call(
+        hand_out,
+        out_shape=tuple(jax.ShapeDtypeStruct(shape, F32) for shape in shapes),
+        in_specs=[vmem] * 3,
+        out_specs=(hbm,) * 3,
+        scratch_shapes=[pltpu.SemaphoreType.DMA((3,))],
+    )(*(pltpu.with_memory_space_constraint(x, pltpu.VMEM) for x in held))
     return lat.reshape(latent_old.shape), coef, res
 
 

time: 53.3 us -> 42.1 us (0.79)
  Pallas kernels: 48 us -> 41.3 us
  local copies, waits for them, and re-layouts: 4.29 us -> 0 us
    pallas_call x1, Pallas kernels: 48 us -> 40.6 us  [per_device(): pl.pallas_call(functools.partial(kernel, n_people, n_var, inverse_root),...]
    unnamed x3 -> x0, local copies, waits for them, and re-layouts: 4.29 us -> none
    pallas_call x0 -> x1, Pallas kernels: none -> 0.74 us  [per_device(): pl.pallas_call(hand_out, out_shape=tuple((jax.ShapeDtypeStruct(shape, F32...]
where the time goes in v2:
time: 42.1 us; the launch traced here: 41.9 us
  Pallas kernels  41.3 us (98%)
  between operations  0.64 us (2%)
    pallas_call x1, Pallas kernels, per_device(): pl.pallas_call(functools.partial(kernel, n_people, n_var, inverse_root),...  40.6 us

profile of v2, /device:TPU:1, one launch (start us, length us, event | category | flops | bytes accessed | tf_op | source)
XLA Modules:
  0.0 41.9 jit_solution(10809544566282452071)
XLA Ops:
  0.6 40.6 %shard_map.94 = (f32[4,128,128]{2,1,0:T(8,128)S(1)}, f32[4,1024]{1,0:T(4,128)S(1)}, f32[4,512]{1,0:T(4,128)S(1)}) custom-call(s32[512,1024]{1,0:T(8,128)} %geno.1, f32[1,1024]{1,0:T(1,128)} %bitcast.9, f32[4,512]{1,0:T(4,128)} %res_h.1, f32[4,128,128]{2,1,0:T(8,128)} %bitcast.6, f32[1,128]{1,0:T(1,128)} %bitcast.10, s32[16,1024]{1,0:T(8,128)} %bitcast.7, ...), custom_call_target="tpu_custom_call" | custom-call | tf_op jit(solution)/shard_map/pallas_call | solution.py:309
  41.2 0.7 %shard_map.95 = (f32[4,128,128]{2,1,0:T(8,128)}, f32[4,1024]{1,0:T(4,128)}, f32[4,512]{1,0:T(4,128)}) custom-call(f32[4,128,128]{2,1,0:T(8,128)S(1)} %get-tuple-element.9.lat, f32[4,1024]{1,0:T(4,128)S(1)} %get-tuple-element.10.coef, f32[4,512]{1,0:T(4,128)S(1)} %get-tuple-element.11.res), custom_call_target="tpu_custom_call" | custom-call | tf_op jit(solution)/shard_map/pallas_call | solution.py:361

commit v3 on v2

--- a/solution.py
+++ b/solution.py
@@ -27,7 +27,7 @@
            lat_out, coef_out, res_out,
            gi, gb, mean, res, lat, weight, source, slot,
            snd, rcv, pc, win, wsum, halves, corr, tables, member, lows,
-           highs, prev, prop, squares, gland, thr, amat, latbuf, latland,
+           highs, prev, prop, squares, gland, thr, amat, cland, own,
            cpart, csib, coef, pland, pbuf,
            in_sems, send_sems, recv_sems):
     p, v = lax.axis_index("people"), lax.axis_index("var")
@@ -39,12 +39,22 @@
     sibling = {"people": p + 1 - 2 * core, "var": v}
     reach = n_z // 4
 
-    def along(d, other=False):
-        return {"people": 2 * lax.rem(z + d + n_z, n_z) + (1 - core if other else core), "var": v}
+    def along(d, on):
+        return {"people": 2 * lax.rem(z + d + n_z, n_z) + on, "var": v}
 
     near = sorted((d for d in range(-reach, reach + 1) if d != 0), key=lambda d: -abs(d))
-    z_peers = [along(d) for d in near] + [along(reach, True), along(-reach, True)]
-    var_peers = [{"people": p, "var": lax.rem(v + d, n_var)} for d in range(1, n_var)]
+    z_peers = [along(d, on) for d in near for on in (0, 1)]
+    side = math.isqrt(n_var)
+    vy, vx = v // side, lax.rem(v, side)
+
+    def in_plane(dy, dx):
+        return {"people": p, "var": lax.rem(vy + dy, side) * side + lax.rem(vx + dx, side)}
+
+    def hops(offset):
+        return sum(min(d, side - d) for d in offset)
+
+    offsets = [(dy, dx) for dy in range(side) for dx in range(side) if dy or dx]
+    var_peers = [in_plane(dy, dx) for dy, dx in sorted(offsets, key=hops, reverse=True)]
 
     def local(src, dst, sem):
         copy = pltpu.make_async_copy(src, dst, sem)
@@ -102,10 +112,14 @@
 
     pl.semaphore_wait(barrier, len(z_peers) + len(var_peers) + 1)
 
-    win[reach] = pc[...]
+    own_rows = pl.ds(pl.multiple_of(16 * core, 16), 16)
+    other_rows = pl.ds(pl.multiple_of(16 - 16 * core, 16), 16)
     for d in near:
         if d < reach:
-            remote(pc, win.at[reach + d], 1, along(-d))
+            for on in (0, 1):
+                remote(pc.at[pl.ds(16 * on, 16), :], win.at[2 * (reach + d) + core], 1, along(-d, on))
+    remote(pc.at[other_rows, :], win.at[2 * reach + core], 1, sibling)
+    win[2 * reach + core] = pc[own_rows, :]
 
     def slab_rows(s):
         return pl.ds(pl.multiple_of(s * LIST_ROWS, 8), LIST_ROWS)
@@ -114,19 +128,18 @@
 
     @pl.when(active)
     def _():
-        for d in range(1, n_var):
-            other = lax.rem(v + d, n_var)
-            remote(snd.at[slab_rows(other), :], rcv.at[mine], 2, {"people": p, "var": other})
+        for device in var_peers:
+            remote(snd.at[slab_rows(device["var"]), :], rcv.at[mine], 2, device)
         rcv[mine] = snd[slab_rows(v), :]
 
-    drain(win.at[pl.ds(0, 2 * reach - 1)], recv_sems.at[1])
+    drain(win.at[pl.ds(0, 4 * reach - 1)], recv_sems.at[1])
     summed = win[0]
-    for k in range(1, 2 * reach):
+    for k in range(1, 4 * reach):
         summed = summed + win[k]
     wsum[...] = summed
     for k, d in enumerate((-reach, reach)):
-        for other in (False, True):
-            remote(wsum, halves.at[2 * core + k], 0, along(d, other))
+        for on in (0, 1):
+            remote(wsum, halves.at[k, own_rows, :], 0, along(d, on))
 
     @pl.when(active)
     def _():
@@ -162,7 +175,7 @@
     lax.fori_loop(0, half, prepare, 0)
 
     drain(halves, recv_sems.at[0])
-    corr[...] = ((halves[0] + halves[1]) + (halves[2] + halves[3])) * inverse_root
+    corr[...] = (halves[0] + halves[1]) * inverse_root
     for t in range(4):
         for h in range(8):
             tables[8 * t + h] = jnp.broadcast_to(corr[8 * t + h:8 * t + h + 1, :], (8, 128))
@@ -192,6 +205,10 @@
     gland[v] = partial
     for device in var_peers:
         remote(gland.at[v], gland.at[v], 3, device)
+
+    cland[v, own_rows, :] = corr[own_rows, :]
+    for device in var_peers:
+        remote(cland.at[v, own_rows, :], cland.at[v, own_rows, :], 5, device)
     drain(gland.at[pl.ds(0, n_var - 1)], recv_sems.at[3])
     norm = gland[0]
     for k in range(1, n_var):
@@ -201,7 +218,12 @@
     shrink = jnp.maximum(norm - threshold, 0.0) / jnp.maximum(norm, threshold)
     squares[0:half, :] = shrink
 
-    slab_place = pl.ds(pl.multiple_of(8 * v, 8), 8)
+    @pl.when(active)
+    def _():
+        own[...] = squares[pl.ds(mine, 1), :]
+        remote(own, own, 7, sibling)
+
+    acc = None
     for o in range(half):
         slots = rcv[o, 40:48, :].astype(jnp.int32)
         live = slots >= 0
@@ -211,7 +233,6 @@
         firsts, seconds = [], []
         for t in range(4):
             fresh = prop[o, 8 * t:8 * t + 8, :] * factor
-            latbuf[o, t] = fresh
             delta = fresh - prev[o, 8 * t:8 * t + 8, :]
             first = delta.astype(BF16).astype(F32)
             firsts.append(first)
@@ -221,21 +242,15 @@
             for k, terms in enumerate((firsts, seconds)):
                 block = jnp.concatenate([mask * term[j:j + 1, :] for term in terms], axis=0)
                 amat[32 * k:32 * k + 32, 1024 * o + 128 * j:1024 * o + 128 * (j + 1)] = block.astype(BF16)
-
-    for o in range(half):
-        owner = core * half + o
-
-        @pl.when(owner != v)
-        def _():
-            remote(latbuf.at[o], latland.at[:, slab_place, :], 5, {"people": p, "var": owner})
-
-    @pl.when(active)
-    def _():
-        latland[:, slab_place, :] = latbuf[mine]
-
-    acc = jnp.dot(amat[...], lows[...], preferred_element_type=F32)
+        if o % 4 == 3:
+            span = slice(1024 * (o - 3), 1024 * (o + 1))
+            part = jnp.dot(amat[:, span], lows[span, :], preferred_element_type=F32)
+            acc = part if acc is None else acc + part
+
     cpart[...] = acc[32:64] + acc[0:32]
     remote(cpart, csib, 4, sibling)
+    drain(cland.at[pl.ds(0, n_var - 1), own_rows, :], recv_sems.at[5])
+    remote(cland.at[:, own_rows, :], cland.at[:, own_rows, :], 8, sibling)
 
     drain(cpart, recv_sems.at[4])
     coef[...] = cpart[...] + csib[...]
@@ -252,16 +267,35 @@
     for device in var_peers:
         remote(pland.at[v], pland.at[v], 6, device)
 
-    @pl.when(active)
-    def _():
-        drain(latland.at[:, pl.ds(0, 8 * (n_var - 1)), :], recv_sems.at[5])
-        remote(latland, latland, 7, sibling)
-
     @pl.when(jnp.logical_not(active))
     def _():
-        drain(latland, recv_sems.at[7])
-
-    lat_out[...] = latland[...]
+        drain(own, recv_sems.at[7])
+
+    drain(cland.at[:, other_rows, :], recv_sems.at[8])
+    own_table = jnp.broadcast_to(own[...], (8, 128))
+
+    def renew(pair, carry):
+        for k in range(2):
+            slab = 2 * pair + k
+            base = pl.multiple_of(slab * LIST_ROWS, 8)
+            sources = snd[pl.ds(base + 32, 8), :].astype(jnp.int32)
+            slots = snd[pl.ds(base + 40, 8), :].astype(jnp.int32)
+            live = slots >= 0
+            group = jnp.where(live, lax.shift_right_arithmetic(slots, 7), 0)
+            factor = jnp.where(live, jnp.take_along_axis(own_table, group, axis=1), 0.0)
+            high = lax.shift_right_arithmetic(sources, 7)
+            low = lax.bitwise_and(sources, 127)
+            for t in range(4):
+                picked = jnp.zeros((8, 128), F32)
+                for h in range(8):
+                    row = jnp.broadcast_to(cland[slab, 8 * t + h:8 * t + h + 1, :], (8, 128))
+                    picked = jnp.where(high == h, jnp.take_along_axis(row, low, axis=1), picked)
+                old = snd[pl.ds(base + 8 * t, 8), :]
+                fresh = (jnp.where(live, old, 0.0) + STEP * jnp.where(live, picked, 0.0)) * factor
+                lat_out[t, pl.ds(pl.multiple_of(8 * slab, 8), 8), :] = fresh
+        return carry
+
+    lax.fori_loop(0, n_var // 2, renew, 0)
 
     drain(pland.at[pl.ds(0, n_var - 1)], recv_sems.at[6])
     predicted = pland[0]
@@ -271,20 +305,17 @@
         res_out[:, 128 * k:128 * (k + 1)] = residual[:, 128 * k:128 * (k + 1)] - predicted[4 * k:4 * k + 4, :] * inverse_root
 
     drain(halves, send_sems.at[0])
-    drain(win.at[pl.ds(0, 2 * reach - 1)], send_sems.at[1])
+    drain(win.at[pl.ds(0, 4 * reach - 1)], send_sems.at[1])
     drain(gland.at[pl.ds(0, n_var - 1)], send_sems.at[3])
     drain(cpart, send_sems.at[4])
+    drain(cland.at[pl.ds(0, n_var - 1), own_rows, :], send_sems.at[5])
+    drain(cland.at[:, own_rows, :], send_sems.at[8])
     drain(pland.at[pl.ds(0, n_var - 1)], send_sems.at[6])
 
     @pl.when(active)
     def _():
         drain(snd.at[pl.ds(0, LIST_ROWS * (n_var - 1)), :], send_sems.at[2])
-        drain(latbuf.at[pl.ds(0, half - 1)], send_sems.at[5])
-        drain(latland, send_sems.at[7])
-
-    @pl.when(jnp.logical_not(active))
-    def _():
-        drain(latbuf, send_sems.at[5])
+        drain(own, send_sems.at[7])
 
 
 def hand_out(lat, coef, res, lat_out, coef_out, res_out, sems):
@@ -323,9 +354,9 @@
             pltpu.VMEM((n_var * LIST_ROWS, 128), F32),
             pltpu.VMEM((half, LIST_ROWS, 128), F32),
             pltpu.VMEM((32, 128), F32),
-            pltpu.VMEM((n_z // 2, 32, 128), F32),
-            pltpu.VMEM((32, 128), F32),
-            pltpu.VMEM((4, 32, 128), F32),
+            pltpu.VMEM((n_z, 16, 128), F32),
+            pltpu.VMEM((16, 128), F32),
+            pltpu.VMEM((2, 32, 128), F32),
             pltpu.VMEM((32, 128), F32),
             pltpu.VMEM((32, 8, 128), F32),
             pltpu.VMEM((half * 128, 1024), BF16),
@@ -337,16 +368,16 @@
             pltpu.VMEM((n_var, half, 128), F32),
             pltpu.VMEM((half, 128), F32),
             pltpu.VMEM((64, half * 1024), BF16),
-            pltpu.VMEM((half, traits, 8, 128), F32),
-            pltpu.VMEM((traits, list_rows, 128), F32),
+            pltpu.VMEM((n_var, 32, 128), F32),
+            pltpu.VMEM((1, 128), F32),
             pltpu.VMEM((32, 128), F32),
             pltpu.VMEM((32, 128), F32),
             pltpu.VMEM((32, 128), F32),
             pltpu.VMEM((n_var, people_dev // 32, 128), F32),
             pltpu.VMEM((people_dev // 32, 128), F32),
             pltpu.SemaphoreType.DMA((10,)),
-            pltpu.SemaphoreType.DMA((8,)),
-            pltpu.SemaphoreType.DMA((8,)),
+            pltpu.SemaphoreType.DMA((9,)),
+            pltpu.SemaphoreType.DMA((9,)),
         ],
         compiler_params=pltpu.CompilerParams(collective_id=0, has_side_effects=True, vmem_limit_bytes=32 * 2**20),
     )(*(pltpu.with_memory_space_constraint(x, pltpu.HBM) for x in (

time: 42.1 us -> 40.6 us (0.964)
  Pallas kernels: 41.3 us -> 39.8 us
    pallas_call x1, Pallas kernels: 40.6 us -> 39.1 us  [per_device(): pl.pallas_call(functools.partial(kernel, n_people, n_var, inverse_root),...]
where the time goes in v3:
time: 40.6 us; the launch traced here: 40.4 us
  Pallas kernels  39.8 us (98%)
  between operations  0.64 us (2%)
    pallas_call x1, Pallas kernels, per_device(): pl.pallas_call(functools.partial(kernel, n_people, n_var, inverse_root),...  39.1 us

profile of v3, /device:TPU:1, one launch (start us, length us, event | category | flops | bytes accessed | tf_op | source)
XLA Modules:
  0.0 40.4 jit_solution(8500536105816273935)
XLA Ops:
  0.6 39.1 %shard_map.94 = (f32[4,128,128]{2,1,0:T(8,128)S(1)}, f32[4,1024]{1,0:T(4,128)S(1)}, f32[4,512]{1,0:T(4,128)S(1)}) custom-call(s32[512,1024]{1,0:T(8,128)} %geno.1, f32[1,1024]{1,0:T(1,128)} %bitcast.9, f32[4,512]{1,0:T(4,128)} %res_h.1, f32[4,128,128]{2,1,0:T(8,128)} %bitcast.6, f32[1,128]{1,0:T(1,128)} %bitcast.10, s32[16,1024]{1,0:T(8,128)} %bitcast.7, ...), custom_call_target="tpu_custom_call" | custom-call | tf_op jit(solution)/shard_map/pallas_call | solution.py:340
  39.7 0.7 %shard_map.95 = (f32[4,128,128]{2,1,0:T(8,128)}, f32[4,1024]{1,0:T(4,128)}, f32[4,512]{1,0:T(4,128)}) custom-call(f32[4,128,128]{2,1,0:T(8,128)S(1)} %get-tuple-element.9.lat, f32[4,1024]{1,0:T(4,128)S(1)} %get-tuple-element.10.coef, f32[4,512]{1,0:T(4,128)S(1)} %get-tuple-element.11.res), custom_call_target="tpu_custom_call" | custom-call | tf_op jit(solution)/shard_map/pallas_call | solution.py:392

commit v4 on v3

--- a/solution.py
+++ b/solution.py
@@ -26,7 +26,7 @@
            geno, mean_h, res_h, lat_h, weight_h, source_h, slot_h,
            lat_out, coef_out, res_out,
            gi, gb, mean, res, lat, weight, source, slot,
-           snd, rcv, pc, win, wsum, halves, corr, tables, member, lows,
+           snd, rcv, pc, spc, win, wsum, halves, corr, tables, member, lows,
            highs, prev, prop, squares, gland, thr, amat, cland, own,
            cpart, csib, coef, pland, pbuf,
            in_sems, send_sems, recv_sems):
@@ -43,7 +43,7 @@
         return {"people": 2 * lax.rem(z + d + n_z, n_z) + on, "var": v}
 
     near = sorted((d for d in range(-reach, reach + 1) if d != 0), key=lambda d: -abs(d))
-    z_peers = [along(d, on) for d in near for on in (0, 1)]
+    z_peers = [along(d, core) for d in near] + [along(d, 1 - core) for d in (reach, -reach)]
     side = math.isqrt(n_var)
     vy, vx = v // side, lax.rem(v, side)
 
@@ -114,13 +114,7 @@
 
     own_rows = pl.ds(pl.multiple_of(16 * core, 16), 16)
     other_rows = pl.ds(pl.multiple_of(16 - 16 * core, 16), 16)
-    for d in near:
-        if d < reach:
-            for on in (0, 1):
-                remote(pc.at[pl.ds(16 * on, 16), :], win.at[2 * (reach + d) + core], 1, along(-d, on))
-    remote(pc.at[other_rows, :], win.at[2 * reach + core], 1, sibling)
-    win[2 * reach + core] = pc[own_rows, :]
-
+    remote(pc.at[other_rows, :], spc, 9, sibling)
     def slab_rows(s):
         return pl.ds(pl.multiple_of(s * LIST_ROWS, 8), LIST_ROWS)
 
@@ -132,9 +126,15 @@
             remote(snd.at[slab_rows(device["var"]), :], rcv.at[mine], 2, device)
         rcv[mine] = snd[slab_rows(v), :]
 
-    drain(win.at[pl.ds(0, 4 * reach - 1)], recv_sems.at[1])
+    drain(spc, recv_sems.at[9])
+    win[reach] = pc[own_rows, :] + spc[...]
+    for d in near:
+        if d < reach:
+            remote(win.at[reach], win.at[reach + d], 1, along(-d, core))
+
+    drain(win.at[pl.ds(0, 2 * reach - 1)], recv_sems.at[1])
     summed = win[0]
-    for k in range(1, 4 * reach):
+    for k in range(1, 2 * reach):
         summed = summed + win[k]
     wsum[...] = summed
     for k, d in enumerate((-reach, reach)):
@@ -305,7 +305,8 @@
         res_out[:, 128 * k:128 * (k + 1)] = residual[:, 128 * k:128 * (k + 1)] - predicted[4 * k:4 * k + 4, :] * inverse_root
 
     drain(halves, send_sems.at[0])
-    drain(win.at[pl.ds(0, 4 * reach - 1)], send_sems.at[1])
+    drain(spc, send_sems.at[9])
+    drain(win.at[pl.ds(0, 2 * reach - 1)], send_sems.at[1])
     drain(gland.at[pl.ds(0, n_var - 1)], send_sems.at[3])
     drain(cpart, send_sems.at[4])
     drain(cland.at[pl.ds(0, n_var - 1), own_rows, :], send_sems.at[5])
@@ -354,7 +355,8 @@
             pltpu.VMEM((n_var * LIST_ROWS, 128), F32),
             pltpu.VMEM((half, LIST_ROWS, 128), F32),
             pltpu.VMEM((32, 128), F32),
-            pltpu.VMEM((n_z, 16, 128), F32),
+            pltpu.VMEM((16, 128), F32),
+            pltpu.VMEM((n_z // 2, 16, 128), F32),
             pltpu.VMEM((16, 128), F32),
             pltpu.VMEM((2, 32, 128), F32),
             pltpu.VMEM((32, 128), F32),
@@ -376,8 +378,8 @@
             pltpu.VMEM((n_var, people_dev // 32, 128), F32),
             pltpu.VMEM((people_dev // 32, 128), F32),
             pltpu.SemaphoreType.DMA((10,)),
-            pltpu.SemaphoreType.DMA((9,)),
-            pltpu.SemaphoreType.DMA((9,)),
+            pltpu.SemaphoreType.DMA((10,)),
+            pltpu.SemaphoreType.DMA((10,)),
         ],
         compiler_params=pltpu.CompilerParams(collective_id=0, has_side_effects=True, vmem_limit_bytes=32 * 2**20),
     )(*(pltpu.with_memory_space_constraint(x, pltpu.HBM) for x in (

time: 40.6 us -> 39.9 us (0.983)
  Pallas kernels: 39.8 us -> 39.1 us
    pallas_call x1, Pallas kernels: 39.1 us -> 38.3 us  [per_device(): pl.pallas_call(functools.partial(kernel, n_people, n_var, inverse_root),...]
where the time goes in v4:
time: 39.9 us; the launch traced here: 39.7 us
  Pallas kernels  39.1 us (98%)
  between operations  0.64 us (2%)
    pallas_call x1, Pallas kernels, per_device(): pl.pallas_call(functools.partial(kernel, n_people, n_var, inverse_root),...  38.3 us

profile of v4, /device:TPU:1, one launch (start us, length us, event | category | flops | bytes accessed | tf_op | source)
XLA Modules:
  0.0 39.7 jit_solution(5000708580004729103)
XLA Ops:
  0.6 38.3 %shard_map.94 = (f32[4,128,128]{2,1,0:T(8,128)S(1)}, f32[4,1024]{1,0:T(4,128)S(1)}, f32[4,512]{1,0:T(4,128)S(1)}) custom-call(s32[512,1024]{1,0:T(8,128)} %geno.1, f32[1,1024]{1,0:T(1,128)} %bitcast.9, f32[4,512]{1,0:T(4,128)} %res_h.1, f32[4,128,128]{2,1,0:T(8,128)} %bitcast.6, f32[1,128]{1,0:T(1,128)} %bitcast.10, s32[16,1024]{1,0:T(8,128)} %bitcast.7, ...), custom_call_target="tpu_custom_call" | custom-call | tf_op jit(solution)/shard_map/pallas_call | solution.py:341
  39.0 0.7 %shard_map.95 = (f32[4,128,128]{2,1,0:T(8,128)}, f32[4,1024]{1,0:T(4,128)}, f32[4,512]{1,0:T(4,128)}) custom-call(f32[4,128,128]{2,1,0:T(8,128)S(1)} %get-tuple-element.9.lat, f32[4,1024]{1,0:T(4,128)S(1)} %get-tuple-element.10.coef, f32[4,512]{1,0:T(4,128)S(1)} %get-tuple-element.11.res), custom_call_target="tpu_custom_call" | custom-call | tf_op jit(solution)/shard_map/pallas_call | solution.py:394

commit v5 on v4

--- a/solution.py
+++ b/solution.py
@@ -176,6 +176,9 @@
 
     drain(halves, recv_sems.at[0])
     corr[...] = (halves[0] + halves[1]) * inverse_root
+    cland[v, own_rows, :] = corr[own_rows, :]
+    for device in var_peers:
+        remote(cland.at[v, own_rows, :], cland.at[v, own_rows, :], 5, device)
     for t in range(4):
         for h in range(8):
             tables[8 * t + h] = jnp.broadcast_to(corr[8 * t + h:8 * t + h + 1, :], (8, 128))
@@ -205,10 +208,6 @@
     gland[v] = partial
     for device in var_peers:
         remote(gland.at[v], gland.at[v], 3, device)
-
-    cland[v, own_rows, :] = corr[own_rows, :]
-    for device in var_peers:
-        remote(cland.at[v, own_rows, :], cland.at[v, own_rows, :], 5, device)
     drain(gland.at[pl.ds(0, n_var - 1)], recv_sems.at[3])
     norm = gland[0]
     for k in range(1, n_var):

time: 39.9 us -> 39.6 us (level)
  no operation moved by 1% of the time
where the time goes in v5:
time: 39.6 us; the launch traced here: 39.4 us
  Pallas kernels  38.8 us (98%)
  between operations  0.64 us (2%)
    pallas_call x1, Pallas kernels, per_device(): pl.pallas_call(functools.partial(kernel, n_people, n_var, inverse_root),...  38 us

profile of v5, /device:TPU:1, one launch (start us, length us, event | category | flops | bytes accessed | tf_op | source)
XLA Modules:
  0.0 39.4 jit_solution(15083538951444100948)
XLA Ops:
  0.6 38.0 %shard_map.94 = (f32[4,128,128]{2,1,0:T(8,128)S(1)}, f32[4,1024]{1,0:T(4,128)S(1)}, f32[4,512]{1,0:T(4,128)S(1)}) custom-call(s32[512,1024]{1,0:T(8,128)} %geno.1, f32[1,1024]{1,0:T(1,128)} %bitcast.9, f32[4,512]{1,0:T(4,128)} %res_h.1, f32[4,128,128]{2,1,0:T(8,128)} %bitcast.6, f32[1,128]{1,0:T(1,128)} %bitcast.10, s32[16,1024]{1,0:T(8,128)} %bitcast.7, ...), custom_call_target="tpu_custom_call" | custom-call | tf_op jit(solution)/shard_map/pallas_call | solution.py:340
  38.7 0.7 %shard_map.95 = (f32[4,128,128]{2,1,0:T(8,128)}, f32[4,1024]{1,0:T(4,128)}, f32[4,512]{1,0:T(4,128)}) custom-call(f32[4,128,128]{2,1,0:T(8,128)S(1)} %get-tuple-element.9.lat, f32[4,1024]{1,0:T(4,128)S(1)} %get-tuple-element.10.coef, f32[4,512]{1,0:T(4,128)S(1)} %get-tuple-element.11.res), custom_call_target="tpu_custom_call" | custom-call | tf_op jit(solution)/shard_map/pallas_call | solution.py:393

commit v6 on v5

--- a/solution.py
+++ b/solution.py
@@ -183,6 +183,7 @@
         for h in range(8):
             tables[8 * t + h] = jnp.broadcast_to(corr[8 * t + h:8 * t + h + 1, :], (8, 128))
 
+    owner_iota = lax.broadcasted_iota(jnp.int32, (4, 128), 0)
     for o in range(half):
         sources = rcv[o, 32:40, :].astype(jnp.int32)
         live = rcv[o, 40:48, :] >= 0.0
@@ -197,15 +198,17 @@
             prop[o, 8 * t:8 * t + 8, :] = value
             total = total + value * value
         squares[8 * o:8 * o + 8, :] = total
-    by_owner = jnp.concatenate([squares[pl.ds(j, half, stride=8), :] for j in range(8)], axis=1)
-    stacked = jnp.concatenate(split3(by_owner), axis=0).astype(BF16)
-    owner_iota = lax.broadcasted_iota(jnp.int32, (half, 128), 0)
-    wide = lax.dot_general(stacked, member[...], (((1,), (1,)), ((), ())), preferred_element_type=F32)
-    wide = wide[2 * half:3 * half] + wide[half:2 * half] + wide[0:half]
-    partial = wide[:, 0:128]
-    for o in range(1, half):
-        partial = jnp.where(owner_iota == o, wide[:, 128 * o:128 * (o + 1)], partial)
-    gland[v] = partial
+        if o % 4 == 3:
+            base = o - 3
+            by_owner = jnp.concatenate([squares[pl.ds(8 * base + j, 4, stride=8), :] for j in range(8)], axis=1)
+            stacked = jnp.concatenate(split3(by_owner), axis=0).astype(BF16)
+            wide = lax.dot_general(stacked, member[128 * base:128 * (base + 4), :], (((1,), (1,)), ((), ())),
+                                   preferred_element_type=F32)
+            wide = wide[8:12] + wide[4:8] + wide[0:4]
+            partial = wide[:, 0:128]
+            for k in range(1, 4):
+                partial = jnp.where(owner_iota == k, wide[:, 128 * k:128 * (k + 1)], partial)
+            gland[v, base:base + 4, :] = partial
     for device in var_peers:
         remote(gland.at[v], gland.at[v], 3, device)
     drain(gland.at[pl.ds(0, n_var - 1)], recv_sems.at[3])

time: 39.6 us -> 39.5 us (level)
  no operation moved by 1% of the time
where the time goes in v6:
time: 39.5 us; the launch traced here: 39.3 us
  Pallas kernels  38.7 us (98%)
  between operations  0.64 us (2%)
    pallas_call x1, Pallas kernels, per_device(): pl.pallas_call(functools.partial(kernel, n_people, n_var, inverse_root),...  38 us

profile of v6, /device:TPU:1, one launch (start us, length us, event | category | flops | bytes accessed | tf_op | source)
XLA Modules:
  0.0 39.3 jit_solution(9762055319399965760)
XLA Ops:
  0.6 38.0 %shard_map.94 = (f32[4,128,128]{2,1,0:T(8,128)S(1)}, f32[4,1024]{1,0:T(4,128)S(1)}, f32[4,512]{1,0:T(4,128)S(1)}) custom-call(s32[512,1024]{1,0:T(8,128)} %geno.1, f32[1,1024]{1,0:T(1,128)} %bitcast.9, f32[4,512]{1,0:T(4,128)} %res_h.1, f32[4,128,128]{2,1,0:T(8,128)} %bitcast.6, f32[1,128]{1,0:T(1,128)} %bitcast.10, s32[16,1024]{1,0:T(8,128)} %bitcast.7, ...), custom_call_target="tpu_custom_call" | custom-call | tf_op jit(solution)/shard_map/pallas_call | solution.py:343
  38.6 0.7 %shard_map.95 = (f32[4,128,128]{2,1,0:T(8,128)}, f32[4,1024]{1,0:T(4,128)}, f32[4,512]{1,0:T(4,128)}) custom-call(f32[4,128,128]{2,1,0:T(8,128)S(1)} %get-tuple-element.9.lat, f32[4,1024]{1,0:T(4,128)S(1)} %get-tuple-element.10.coef, f32[4,512]{1,0:T(4,128)S(1)} %get-tuple-element.11.res), custom_call_target="tpu_custom_call" | custom-call | tf_op jit(solution)/shard_map/pallas_call | solution.py:396
